TPU v7x, 32 devices: a whole 2x2x4 slice. The times are simulated.
32 devices in a mesh: groups: 2 (over x), row: 8 (over z, y), col: 2 (over core).
Axes of the slice: x: 2, y: 2, z: 4, core: 2. Of those that a mesh axis runs over, the one named last changes fastest.
Arguments:
- pair: bfloat16 [384, 192, 128], P(('groups', 'row'), 'col'), parts along dimension 0, may hold values from -6 to 6
- mask: int32 [384, 192], P(('groups', 'row'), 'col'), parts along dimension 0, may hold values from 0 to 1, as said below
- w_in: bfloat16 [2, 128, 512], replicated, may hold values from -0.5 to 0.5
- w_gate: bfloat16 [2, 128, 128], replicated, may hold values from -0.5 to 0.5
- w_out: bfloat16 [2, 128, 128], replicated, may hold values from -0.5 to 0.5
Outputs:
- pair_out: bfloat16 [384, 192, 128], P(('groups', 'row'), 'col'), parts along dimension 0
There are 2 independent parts, one for each index of `groups`. A program takes and returns all parts, laid end to end along the dimension named above; an argument that names none is the same for every part. Nothing has to cross between parts.
Inputs may be any that keep to these rules, and one draw needn't show every extreme that they name: mask[i][j] is 1 exactly when residues i and j are both real. The residues fall into four chain slots of 48 in order; in each slot the real residues run from the slot's start for the chain's length, at least 24, and the rest are padding.
All inputs are finite; a program needn't handle non-finite values.
Results may differ from a plain program's by a relative error of at most 0.012.
Values may be sent and summed in bfloat16 or wider, within the bound.
A program may use at most 128 MiB of HBM per device.

v0:
```python
import jax
import jax.numpy as jnp
from jax import lax
from jax.sharding import PartitionSpec as P


def layer_norm(values, dimension):
    average = jnp.mean(values, axis=dimension, keepdims=True)
    centered = values - average
    variance = jnp.mean(centered * centered, axis=dimension, keepdims=True)
    return centered * lax.rsqrt(variance + 1e-05)


def triangle(pair_in, mask_flat, weight_in, weight_gate, weight_out, outgoing):
    tile_rows, tile_cols, channels = pair_in.shape
    pair_count = tile_rows * tile_cols
    hidden = weight_in.shape[1] // 4
    row_count = lax.axis_size("row")
    col_count = lax.axis_size("col")
    groups = row_count * col_count
    per_group = hidden // groups
    flat_pair = pair_in.reshape(pair_count, channels).astype(jnp.float32)
    normed = layer_norm(flat_pair, 1).astype(jnp.bfloat16)
    projected = jnp.einsum("pc,ch->hp", normed, weight_in, preferred_element_type=jnp.float32)
    stacked = (
        mask_flat[None, :] * jax.nn.sigmoid(projected[: 2 * hidden]) * projected[2 * hidden :]
    ).astype(jnp.bfloat16)
    stacked = stacked.reshape(2, groups, per_group, pair_count)
    equation = "mik,mjk->mij" if outgoing else "mki,mkj->mij"
    pieces = lax.all_to_all(stacked, ("row", "col"), split_axis=1, concat_axis=1, tiled=True)
    item_count = pieces.shape[2]
    gathered = pieces.reshape(2, row_count, col_count, item_count, tile_rows, tile_cols)
    gathered = jnp.transpose(gathered, (0, 3, 1, 4, 2, 5))
    gathered = gathered.reshape(2, item_count, row_count * tile_rows, col_count * tile_cols)
    product = jnp.einsum(
        equation, gathered[0], gathered[1], preferred_element_type=jnp.float32
    ).astype(jnp.bfloat16)
    product = product.reshape(item_count, row_count, tile_rows, col_count, tile_cols)
    product = jnp.transpose(product, (1, 3, 0, 2, 4))
    result = lax.all_to_all(
        product.reshape(groups, item_count, pair_count),
        ("row", "col"),
        split_axis=0,
        concat_axis=0,
        tiled=True,
    )
    result = result.reshape(hidden, pair_count)
    mixed_norm = layer_norm(result.astype(jnp.float32), 0).astype(jnp.bfloat16)
    update = jnp.einsum("hp,hc->pc", mixed_norm, weight_out, preferred_element_type=jnp.float32)
    gate_value = jax.nn.sigmoid(jnp.dot(normed, weight_gate, preferred_element_type=jnp.float32))
    output = (flat_pair + gate_value * update).astype(jnp.bfloat16)
    return output.reshape(tile_rows, tile_cols, channels)


def per_device(pair, mask, w_in, w_gate, w_out):
    mask_flat = mask.reshape(-1).astype(jnp.float32)
    first = triangle(pair, mask_flat, w_in[0], w_gate[0], w_out[0], True)
    return triangle(first, mask_flat, w_in[1], w_gate[1], w_out[1], False)


def solution(mesh):
    placed = (P(("groups", "row"), "col", None), P(("groups", "row"), "col"), P(), P(), P())
    return jax.shard_map(
        per_device,
        mesh=mesh,
        in_specs=placed,
        out_specs=P(("groups", "row"), "col", None),
        check_vma=False,
    )
```

profile of v0, /device:TPU:0, one launch (start us, length us, event | category | flops | bytes accessed | tf_op | source)
XLA Modules:
  0.0 146.0 jit_solution(5160114640651233551)
XLA Ops:
  0.0 1.4 convert_reduce_fusion.2
  1.4 1.9 %multiply_reduce_fusion.1 = f32[24,96]{1,0:T(8,128)S(1)} fusion(bf16[24,96,128]{2,1,0:T(8,128)(2,1)} %param.5, f32[24,96]{1,0:T(8,128)S(1)} %broadcast_multiply_fusion.3), kind=kLoop, calls=%fused_computation.49 | loop fusion | flops 1177344 | bytes 608256 | tf_op jit(solution)/shard_map/reduce_sum | solution.py:10
  3.3 0.8 multiply_convert_fusion.1
  4.3 0.8 convolution_bitcast_fusion.1
  5.1 0.6 fusion.16
  5.8 36.7 %all_to_all.20 = bf16[2,16,8,2304]{3,2,0,1:T(8,128)(2,1)S(1)} all-to-all(bf16[2,16,8,2304]{3,2,0,1:T(8,128)(2,1)S(1)} %copy.19), channel_id=1, replica_groups=mesh['groups'=2,'row'=8,'col'=2] {'row','col'}, dimensions={1} | all-to-all | bytes 2359296 | tf_op jit(solution)/shard_map/all_to_all | solution.py:30
  42.5 2.4 %reshape.163 = bf16[2,8,2,8,24,96]{5,4,3,0,2,1:T(8,128)(2,1)S(1)} reshape(bf16[2,16,8,2304]{3,2,0,1:T(8,128)(2,1)S(1)} %all_to_all.20) | data formatting | bytes 2359296 | tf_op jit(solution)/shard_map/reshape | solution.py:32
  44.9 2.4 %copy.32 = bf16[2,8,2,8,24,96]{5,2,4,1,3,0:T(2,128)(2,1)S(1)} copy(bf16[2,8,2,8,24,96]{5,4,3,0,2,1:T(8,128)(2,1)S(1)} %reshape.163) | data formatting | bytes 2359296 | tf_op jit(solution)/shard_map/reshape | solution.py:32
  47.3 1.2 fusion.50
  49.4 1.3 convolution_convert_fusion.1
  50.7 2.4 %reshape.164 = bf16[8,8,24,2,96]{4,3,2,1,0:T(2,128)(2,1)S(1)} reshape(bf16[8,192,192]{2,1,0:T(8,128)(2,1)} %convolution_convert_fusion.1) | data formatting | bytes 1179648 | tf_op jit(solution)/shard_map/reshape | solution.py:38
  53.3 1.4 reshape.165
  54.7 3.8 %all-to-all-start.1 = ((bf16[16,8,2304]{2,1,0:T(8,128)(2,1)}), bf16[16,8,2304]{2,1,0:T(8,128)(2,1)S(1)}, u32[]{:S(2)}, u32[]{:S(2)}) async-start(bf16[16,8,2304]{2,1,0:T(8,128)(2,1)} %reshape.165), calls=%async_computation.1 | async-start | bytes 1179648 | tf_op jit(solution)/shard_map/all_to_all | solution.py:40
  59.0 14.8 %all-to-all-done.1 = bf16[16,8,2304]{2,1,0:T(8,128)(2,1)S(1)} async-done(((bf16[16,8,2304]{2,1,0:T(8,128)(2,1)}), bf16[16,8,2304]{2,1,0:T(8,128)(2,1)S(1)}, u32[]{:S(2)}, u32[]{:S(2)}) %all-to-all-start.1) | async-done | bytes 589856 | tf_op jit(solution)/shard_map/all_to_all | solution.py:40
  74.7 0.6 fusion.51
  75.3 0.7 multiply_reduce_fusion
  76.2 1.1 convolution_bitcast_fusion
  77.3 0.6 fusion.11
  78.0 33.6 %all_to_all.21 = bf16[2,16,8,2304]{3,2,0,1:T(8,128)(2,1)S(1)} all-to-all(bf16[2,16,8,2304]{3,2,0,1:T(8,128)(2,1)S(1)} %copy.22), channel_id=1, replica_groups=mesh['groups'=2,'row'=8,'col'=2] {'row','col'}, dimensions={1} | all-to-all | bytes 2359296 | tf_op jit(solution)/shard_map/all_to_all | solution.py:30
  111.6 1.1 copy.23
  112.7 3.6 %reshape.167 = bf16[2,8,2,8,24,96]{5,4,3,2,1,0:T(8,128)(2,1)S(1)} reshape(bf16[2,16,8,2304]{3,2,1,0:T(8,128)(2,1)} %copy.23) | data formatting | bytes 2359296 | tf_op jit(solution)/shard_map/reshape | solution.py:32
  116.3 1.2 fusion.49
  117.5 0.8 copy.24
  118.3 1.3 squeeze.37
  119.7 0.8 copy.25
  120.5 1.4 squeeze.38
  121.8 1.6 %convolution_convert_fusion = bf16[8,192,192]{2,1,0:T(8,128)(2,1)S(1)} fusion(bf16[8,192,192]{2,1,0:T(8,128)(2,1)S(1)} %copy-done.2, bf16[8,192,192]{2,1,0:T(8,128)(2,1)} %squeeze.38), kind=kOutput, calls=%fused_computation.40 | convolution fusion | flops 113541120 | bytes 1769472 | tf_op jit(solution)/shard_map/mki,mkj->mij/dot_general | solution.py:35
  124.0 1.4 reshape.169
  125.5 3.6 %all-to-all-start.3 = ((bf16[16,8,2304]{2,1,0:T(8,128)(2,1)}), bf16[16,8,2304]{2,1,0:T(8,128)(2,1)S(1)}, u32[]{:S(2)}, u32[]{:S(2)}) async-start(bf16[16,8,2304]{2,1,0:T(8,128)(2,1)} %reshape.169), calls=%async_computation.3 | async-start | bytes 1179648 | tf_op jit(solution)/shard_map/all_to_all | solution.py:40
  129.1 0.8 fusion.4
  129.9 14.7 %all-to-all-done.3 = bf16[16,8,2304]{2,1,0:T(8,128)(2,1)S(1)} async-done(((bf16[16,8,2304]{2,1,0:T(8,128)(2,1)}), bf16[16,8,2304]{2,1,0:T(8,128)(2,1)S(1)}, u32[]{:S(2)}, u32[]{:S(2)}) %all-to-all-start.3) | async-done | bytes 589856 | tf_op jit(solution)/shard_map/all_to_all | solution.py:40
  144.9 1.2 fusion.10
  (46 shorter events, 3.7 us)
Async XLA Ops:
  0.0 3.3 %copy-start = (bf16[24,96,128]{2,1,0:T(8,128)(2,1)S(1)}, bf16[24,96,128]{2,1,0:T(8,128)(2,1)}, u32[]{:S(2)}) copy-start(bf16[24,96,128]{2,1,0:T(8,128)(2,1)} %param.5) | copy-start | bytes 1769476
  0.0 4.2 %copy-start.9 = (s32[24,96]{1,0:T(8,128)S(1)}, s32[24,96]{1,0:T(8,128)}, u32[]{:S(2)}) copy-start(s32[24,96]{1,0:T(8,128)} %param.6) | copy-start | bytes 27652
  0.0 4.3 %copy-start.5 = (bf16[2,128,512]{2,1,0:T(8,128)(2,1)S(1)}, bf16[2,128,512]{2,1,0:T(8,128)(2,1)}, u32[]{:S(2)}) copy-start(bf16[2,128,512]{2,1,0:T(8,128)(2,1)} %param.7) | copy-start | bytes 786436
  4.2 0.9 copy-start.3
  53.3 5.2 %copy-start.4 = (bf16[24,96,128]{2,1,0:T(8,128)(2,1)S(1)}, bf16[24,96,128]{2,1,0:T(8,128)(2,1)}, u32[]{:S(2)}) copy-start(bf16[24,96,128]{2,1,0:T(8,128)(2,1)} %copy-done.3) | copy-start | bytes 1769476
  53.3 5.2 %copy-start.10 = (bf16[2,128,128]{2,1,0:T(8,128)(2,1)S(1)}, bf16[2,128,128]{2,1,0:T(8,128)(2,1)}, u32[]{:S(2)}) copy-start(bf16[2,128,128]{2,1,0:T(8,128)(2,1)} %param.8) | copy-start | bytes 196612
  54.7 19.1 %all-to-all-start.1 = ((bf16[16,8,2304]{2,1,0:T(8,128)(2,1)}), bf16[16,8,2304]{2,1,0:T(8,128)(2,1)S(1)}, u32[]{:S(2)}, u32[]{:S(2)}) async-start(bf16[16,8,2304]{2,1,0:T(8,128)(2,1)} %reshape.165), calls=%async_computation.1 | async-start | bytes 1179648 | tf_op jit(solution)/shard_map/all_to_all | solution.py:40
  73.8 0.8 copy-start.7
  75.3 1.0 copy-start.6
  118.3 1.3 copy-start.1
  120.5 1.4 copy-start.2
  124.0 5.0 %copy-start.11 = (bf16[2,128,128]{2,1,0:T(8,128)(2,1)S(1)}, bf16[2,128,128]{2,1,0:T(8,128)(2,1)}, u32[]{:S(2)}) copy-start(bf16[2,128,128]{2,1,0:T(8,128)(2,1)} %param.8) | copy-start | bytes 196612
  125.5 19.1 %all-to-all-start.3 = ((bf16[16,8,2304]{2,1,0:T(8,128)(2,1)}), bf16[16,8,2304]{2,1,0:T(8,128)(2,1)S(1)}, u32[]{:S(2)}, u32[]{:S(2)}) async-start(bf16[16,8,2304]{2,1,0:T(8,128)(2,1)} %reshape.169), calls=%async_computation.3 | async-start | bytes 1179648 | tf_op jit(solution)/shard_map/all_to_all | solution.py:40
  129.9 15.0 %copy-start.8 = (bf16[2,128,128]{2,1,0:T(8,128)(2,1)S(1)}, bf16[2,128,128]{2,1,0:T(8,128)(2,1)}, u32[]{:S(2)}) copy-start(bf16[2,128,128]{2,1,0:T(8,128)(2,1)} %param.9) | copy-start | bytes 196612
where the time goes:
time: 147 us; the launch traced here: 146 us
  blocking collectives  70.3 us (48%)
  waiting for transfers between devices  29.5 us (20%)
  local copies, waits for them, and re-layouts  24.1 us (16%)
  matrix products  7.81 us (5%)
  starting transfers between devices  7.35 us (5%)
  other arithmetic  6.64 us (5%)
    all_to_all x2, blocking collectives, triangle(): lax.all_to_all(stacked, ('row', 'col'), split_axis=1, concat_axis=1, tile...  70.3 us
    all_to_all x2, waiting for transfers between devices, triangle(): lax.all_to_all(product.reshape(groups, item_count, pair_count), ('row', '...  29.5 us
    reshape x3, local copies, waits for them, and re-layouts, triangle(): pieces.reshape(2, row_count, col_count, item_count, tile_rows, tile_cols)  8.4 us
    all_to_all x2, starting transfers between devices, triangle(): lax.all_to_all(product.reshape(groups, item_count, pair_count), ('row', '...  7.35 us
    slice x3, local copies, waits for them, and re-layouts, triangle(): gathered[1]  3.17 us
    reshape x4, local copies, waits for them, and re-layouts, triangle(): product.reshape(item_count, row_count, tile_rows, col_count, tile_cols)  3.11 us
  transfers between devices with their start and end apart: 2, of which 2 were waited for; matrix products, arithmetic and copies ran while one was open for 1% of the time, Pallas kernels for 0%

commit v1 on v0

--- a/solution.py
+++ b/solution.py
@@ -1,7 +1,13 @@
+import functools
+
 import jax
 import jax.numpy as jnp
 from jax import lax
+from jax.experimental import pallas as pl
+from jax.experimental.pallas import tpu as pltpu
 from jax.sharding import PartitionSpec as P
+
+LANES = 128
 
 
 def layer_norm(values, dimension):
@@ -52,8 +58,293 @@
     return output.reshape(tile_rows, tile_cols, channels)
 
 
+def flip(index, step, count):
+    total, bit = 0, 1
+    while bit < count:
+        total = total + ((index // bit + step // bit) % 2) * bit
+        bit *= 2
+    return total
+
+
+def step_order(count):
+    half = count // 2
+    return [half + k // 2 if k % 2 == 0 else (k // 2 + 1) % half for k in range(count)]
+
+
+def fused_kernel(
+    outgoing, rows, cols, T, W,
+    z_ref, mask_ref, win_ref, wgate_ref, wout_ref, out_ref,
+    normed, normed_t, gate, send1, recv1, pairs, mix, send2, recv2, mixed_t,
+    send_sem1, recv_sem1, send_sem2, recv_sem2,
+):
+    D = rows * cols
+    count = T * W
+    C = z_ref.shape[1]
+    owned = recv1.shape[1] // 2
+    N = rows * T
+    per_col = N // cols
+    me = lax.axis_index("row") * cols + lax.axis_index("col")
+    order = step_order(D)
+    lane = lax.broadcasted_iota(jnp.int32, (1, LANES), 1)
+
+    def device(step):
+        other = flip(me, step, D)
+        return {"row": other // cols, "col": other % cols}
+
+    barrier = pltpu.get_barrier_semaphore()
+    for step in range(1, D):
+        pl.semaphore_signal(
+            barrier, inc=1, device_id=device(step), device_id_type=pl.DeviceIdType.MESH
+        )
+
+    chunk = 384
+    chunks = count // chunk
+
+    def normalize(part, carry):
+        at = pl.ds(pl.multiple_of(part * chunk, chunk), chunk)
+        values = z_ref[at, :].astype(jnp.float32)
+        centered = values - jnp.mean(values, axis=1, keepdims=True)
+        variance = jnp.mean(centered * centered, axis=1, keepdims=True)
+        result = centered * lax.rsqrt(variance + 1e-05)
+        normed[at, :] = result.astype(jnp.bfloat16)
+        normed_t[:, at] = result.T.astype(jnp.bfloat16)
+        return carry
+
+    lax.fori_loop(0, chunks, normalize, 0)
+    pl.semaphore_wait(barrier, D - 1)
+
+    def copy1(step):
+        return pltpu.make_async_remote_copy(
+            src_ref=send1.at[step],
+            dst_ref=recv1.at[step],
+            send_sem=send_sem1.at[step],
+            recv_sem=recv_sem1.at[step],
+            device_id=device(step),
+            device_id_type=pl.DeviceIdType.MESH,
+        )
+
+    def copy2(step):
+        return pltpu.make_async_remote_copy(
+            src_ref=send2.at[step],
+            dst_ref=recv2.at[step],
+            send_sem=send_sem2.at[step],
+            recv_sem=recv_sem2.at[step],
+            device_id=device(step),
+            device_id_type=pl.DeviceIdType.MESH,
+        )
+
+    bundle = 4
+    wide = 768
+    for first in range(0, D, bundle):
+        steps = order[first : first + bundle]
+        weights = jnp.concatenate([win_ref[flip(me, step, D)] for step in steps], axis=0)
+        for start in range(0, count, wide):
+            here = pl.ds(start, wide)
+            projected = jnp.dot(weights, normed_t[:, here], preferred_element_type=jnp.float32)
+            for place, step in enumerate(steps):
+                base = place * 4 * owned
+                gates = projected[base : base + 2 * owned]
+                values = projected[base + 2 * owned : base + 4 * owned]
+                opened = 0.5 + 0.5 * jnp.tanh(0.5 * gates)
+                target = recv1 if step == 0 else send1
+                target[step, :, here] = (mask_ref[:, here] * opened * values).astype(jnp.bfloat16)
+        for step in steps:
+            if step:
+                copy1(step).start()
+
+    def open_gate(part, carry):
+        at = pl.ds(pl.multiple_of(part * chunk, chunk), chunk)
+        logits = jnp.dot(normed[at, :], wgate_ref[...], preferred_element_type=jnp.float32)
+        gate[at, :] = 0.5 + 0.5 * jnp.tanh(0.5 * logits)
+        return carry
+
+    lax.fori_loop(0, chunks, open_gate, 0)
+
+    def spread(step):
+        source = flip(me, step, D)
+        block, half = source // cols, source % cols
+        for four in range(T // 4):
+            v = [
+                recv1[step, :, pl.ds((3 * four + i) * LANES, LANES)].astype(jnp.float32)
+                for i in range(3)
+            ]
+            pieces = [
+                v[0],
+                jnp.where(lane < 32, pltpu.roll(v[0], 32, 1), pltpu.roll(v[1], 32, 1)),
+                jnp.where(lane < 64, pltpu.roll(v[1], 64, 1), pltpu.roll(v[2], 64, 1)),
+                pltpu.roll(v[2], 96, 1),
+            ]
+            for i, piece in enumerate(pieces):
+                pairs[half, block, pl.ds(4 * four + i, 2 * owned, stride=T), :] = jnp.where(
+                    lane < W, piece, 0.0
+                )
+
+    spread(0)
+
+    def receive(k, carry):
+        step = jnp.where(k % 2 == 0, D // 2 + k // 2, (k // 2 + 1) % (D // 2))
+        copy1(step).wait_recv()
+        spread(step)
+        return carry
+
+    lax.fori_loop(0, D - 1, receive, 0)
+
+    def channel(which, half):
+        block = pairs[half, :, pl.ds(which * T, T), :]
+        return block.reshape(N, LANES).astype(jnp.bfloat16)
+
+    for h in range(owned):
+        left = jnp.concatenate([channel(h, half) for half in range(cols)], axis=1)
+        right = jnp.concatenate([channel(owned + h, half) for half in range(cols)], axis=1)
+        if outgoing:
+            blank = jnp.zeros((LANES - per_col, cols * LANES), jnp.bfloat16)
+            parts = []
+            for half in range(cols):
+                parts += [right[half * per_col : (half + 1) * per_col], blank]
+            right = jnp.concatenate(parts, axis=0)
+            product = lax.dot_general(
+                left, right, (((1,), (1,)), ((), ())), preferred_element_type=jnp.float32
+            )
+        else:
+            product = lax.dot_general(
+                left, right, (((0,), (0,)), ((), ())), preferred_element_type=jnp.float32
+            )
+        for block in range(rows):
+            at = block * T
+            if not outgoing:
+                at = at // per_col * LANES + at % per_col
+            for half in range(cols):
+                mix[block, half, pl.ds(h * T, T), :] = product[
+                    at : at + T, half * LANES : (half + 1) * LANES
+                ]
+
+    def pack(step, target):
+        other = flip(me, step, D)
+        block, half = other // cols, other % cols
+        for four in range(T // 8):
+            both = []
+            for upper in range(2):
+                row = upper * (T // 2) + 4 * four
+                p = [
+                    mix[block, half, pl.ds(row + i, owned, stride=T), :] for i in range(4)
+                ]
+                one, two, three = pltpu.roll(p[1], 96, 1), pltpu.roll(p[2], 64, 1), pltpu.roll(p[3], 32, 1)
+                both.append([
+                    jnp.where(lane < 96, p[0], one),
+                    jnp.where(lane < 64, one, two),
+                    jnp.where(lane < 32, two, three),
+                ])
+            for i in range(3):
+                target[step, :, pl.ds((3 * four + i) * LANES, LANES)] = jnp.concatenate(
+                    [both[0][i], both[1][i]], axis=0
+                ).astype(jnp.bfloat16)
+
+    def give(k, carry):
+        step = jnp.where(k % 2 == 0, D // 2 + k // 2, (k // 2 + 1) % (D // 2))
+        pack(step, send2)
+        copy2(step).start()
+        return carry
+
+    lax.fori_loop(0, D - 1, give, 0)
+    pack(0, recv2)
+
+    def collect(step):
+        owner = flip(me, step, D)
+        values = recv2[step].astype(jnp.float32)
+        mixed_t[owner, :, : count // 2] = values[:owned]
+        mixed_t[owner, :, count // 2 :] = values[owned:]
+
+    collect(0)
+
+    def take(k, carry):
+        step = jnp.where(k % 2 == 0, D // 2 + k // 2, (k // 2 + 1) % (D // 2))
+        copy2(step).wait_recv()
+        collect(step)
+        return carry
+
+    lax.fori_loop(0, D - 1, take, 0)
+
+    def finish(part, carry):
+        at = pl.ds(pl.multiple_of(part * chunk, chunk), chunk)
+        values = mixed_t[:, :, at].reshape(D * owned, chunk)
+        centered = values - jnp.mean(values, axis=0, keepdims=True)
+        variance = jnp.mean(centered * centered, axis=0, keepdims=True)
+        mixed_norm = (centered * lax.rsqrt(variance + 1e-05)).T.astype(jnp.bfloat16)
+        update = jnp.dot(mixed_norm, wout_ref[...], preferred_element_type=jnp.float32)
+        out_ref[at, :] = (z_ref[at, :].astype(jnp.float32) + gate[at, :] * update).astype(jnp.bfloat16)
+        return carry
+
+    lax.fori_loop(0, chunks, finish, 0)
+
+    def settle(step, carry):
+        copy1(step).wait_send()
+        copy2(step).wait_send()
+        return carry
+
+    lax.fori_loop(1, D, settle, 0)
+
+
+def fused_triangle(flat, mask_flat, weight_in, weight_gate, weight_out, outgoing, T, W):
+    rows, cols = lax.axis_size("row"), lax.axis_size("col")
+    D = rows * cols
+    count, C = flat.shape
+    owned = weight_in.shape[1] // 4
+    vmem = pltpu.VMEM
+    return pl.pallas_call(
+        functools.partial(fused_kernel, outgoing, rows, cols, T, W),
+        out_shape=jax.ShapeDtypeStruct((count, C), jnp.bfloat16),
+        in_specs=[pl.BlockSpec(memory_space=vmem)] * 5,
+        out_specs=pl.BlockSpec(memory_space=vmem),
+        scratch_shapes=[
+            vmem((count, C), jnp.bfloat16),
+            vmem((C, count), jnp.bfloat16),
+            vmem((count, C), jnp.float32),
+            vmem((D, 2 * owned, count), jnp.bfloat16),
+            vmem((D, 2 * owned, count), jnp.bfloat16),
+            vmem((cols, rows, 2 * owned * T, LANES), jnp.float32),
+            vmem((rows, cols, owned * T, LANES), jnp.float32),
+            vmem((D, 2 * owned, count // 2), jnp.bfloat16),
+            vmem((D, 2 * owned, count // 2), jnp.bfloat16),
+            vmem((D, owned, count), jnp.float32),
+            pltpu.SemaphoreType.DMA((D,)),
+            pltpu.SemaphoreType.DMA((D,)),
+            pltpu.SemaphoreType.DMA((D,)),
+            pltpu.SemaphoreType.DMA((D,)),
+        ],
+        compiler_params=pltpu.CompilerParams(
+            collective_id=0 if outgoing else 1,
+            has_side_effects=True,
+            vmem_limit_bytes=48 * 1024 * 1024,
+        ),
+    )(flat, mask_flat, weight_in, weight_gate, weight_out)
+
+
+def fits_fused(pair, w_in):
+    rows, cols = lax.axis_size("row"), lax.axis_size("col")
+    D = rows * cols
+    T, W, C = pair.shape
+    H = w_in.shape[2] // 4
+    return (
+        W == 96 and T % 8 == 0 and cols == 2 and D & (D - 1) == 0
+        and C == LANES and H == LANES and H == 8 * D and rows * T == cols * W
+    )
+
+
 def per_device(pair, mask, w_in, w_gate, w_out):
     mask_flat = mask.reshape(-1).astype(jnp.float32)
+    if fits_fused(pair, w_in):
+        T, W, C = pair.shape
+        D = lax.axis_size("row") * lax.axis_size("col")
+        H = w_in.shape[2] // 4
+        by_owner = w_in.reshape(2, C, 4, D, H // D)
+        by_owner = jnp.transpose(by_owner, (0, 3, 2, 4, 1)).reshape(2, D, 4 * H // D, C)
+        values = pair.reshape(T * W, C)
+        for update in range(2):
+            values = fused_triangle(
+                values, mask_flat[None, :], by_owner[update], w_gate[update], w_out[update],
+                update == 0, T, W,
+            )
+        return values.reshape(T, W, C)
     first = triangle(pair, mask_flat, w_in[0], w_gate[0], w_out[0], True)
     return triangle(first, mask_flat, w_in[1], w_gate[1], w_out[1], False)
 

time: 147 us -> 101 us (0.69)
  Pallas kernels: 0 us -> 96.9 us
  blocking collectives: 70.3 us -> 0 us
  waiting for transfers between devices: 29.5 us -> 0 us
  local copies, waits for them, and re-layouts: 24.1 us -> 2.95 us
  matrix products: 7.81 us -> 0 us
  starting transfers between devices: 7.35 us -> 0 us
  other arithmetic: 6.64 us -> 0.75 us
    pallas_call x0 -> x2, Pallas kernels: none -> 96.9 us  [fused_triangle(): pl.pallas_call(functools.partial(fused_kernel, outgoing, rows, cols, T, W...]
    all_to_all x2 -> x0, blocking collectives: 70.3 us -> none  [triangle(): lax.all_to_all(stacked, ('row', 'col'), split_axis=1, concat_axis=1, tile...]
    all_to_all x2 -> x0, waiting for transfers between devices: 29.5 us -> none  [triangle(): lax.all_to_all(product.reshape(groups, item_count, pair_count), ('row', '...]
    reshape x11 -> x0, local copies, waits for them, and re-layouts: 14.5 us -> none  [the longest x3 8.4 us: triangle(): pieces.reshape(2, row_count, col_count, item_count, tile_rows, tile_cols)]
    dot_general x8 -> x0, matrix products: 7.81 us -> none  [the longest x2 2.88 us: triangle(): jnp.einsum(equation, gathered[0], gathered[1], preferred_element_type=jnp...]
    all_to_all x2 -> x0, starting transfers between devices: 7.35 us -> none  [triangle(): lax.all_to_all(product.reshape(groups, item_count, pair_count), ('row', '...]
    reduce_sum x7 -> x0, other arithmetic: 4.52 us -> none  [the longest x4 2.91 us: layer_norm(): variance = jnp.mean(centered * centered, axis=dimension, keepdims=True)]
    slice x4 -> x1, local copies, waits for them, and re-layouts: 3.98 us -> 0.02 us  [per_device(): by_owner[update]]
  transfers between devices with their start and end apart: 2 -> 0, of which waited for: 2 -> 0; matrix products, arithmetic and copies ran while one was open for 1% -> 0% of each run, Pallas kernels for 0% -> 0%
where the time goes in v1:
time: 101 us
  Pallas kernels  96.9 us (96%)
  local copies, waits for them, and re-layouts  2.95 us (3%)
    pallas_call x2, Pallas kernels, fused_triangle(): pl.pallas_call(functools.partial(fused_kernel, outgoing, rows, cols, T, W...  96.9 us

profile of v1, /device:TPU:0, one launch (start us, length us, event | category | flops | bytes accessed | tf_op | source)
XLA Modules:
  0.0 100.7 jit_solution(5020174390579494989)
XLA Ops:
  0.0 0.0 copy-start.1
  0.0 0.8 convert_element_type.13
  0.8 0.1 convert_element_type.14.mask_ref
  0.8 0.8 slice_bitcast_fusion
  1.7 0.0 copy-done.1
  1.7 0.2 copy.7
  1.9 0.0 copy-start
  1.9 1.0 copy-done
  2.9 50.6 %shard_map.55.z_ref = bf16[2304,128]{1,0:T(8,128)(2,1)S(1)} custom-call(bf16[2304,128]{1,0:T(8,128)(2,1)S(1)} %bitcast.18, f32[1,2304]{1,0:T(1,128)S(1)} %convert_element_type.14.mask_ref, bf16[16,32,128]{2,1,0:T(8,128)(2,1)S(1)} %get-tuple-element.12.win_ref, bf16[128,128]{1,0:T(8,128)(2,1)S(1)} %get-tuple-element.13.wgate_ref, ...), custom_call_target="tpu_custom_call" | custom-call | tf_op jit(solution)/shard_map/pallas_call | solution.py:293
  53.5 46.3 %shard_map.56 = bf16[2304,128]{1,0:T(8,128)(2,1)S(1)} custom-call(bf16[2304,128]{1,0:T(8,128)(2,1)S(1)} %shard_map.55.z_ref, f32[1,2304]{1,0:T(1,128)S(1)} %convert_element_type.14.mask_ref, bf16[16,32,128]{2,1,0:T(8,128)(2,1)S(1)} %get-tuple-element.11.win_ref, bf16[128,128]{1,0:T(8,128)(2,1)S(1)} %get-tuple-element.14.wgate_ref, ...), custom_call_target="tpu_custom_call" | custom-call | tf_op jit(solution)/shard_map/pallas_call | solution.py:293
  99.8 0.8 copy.13
  (2 shorter events, 0.1 us)
Async XLA Ops:
  0.0 1.7 %copy-start.1 = (bf16[2,128,512]{2,1,0:T(8,128)(2,1)S(1)}, bf16[2,128,512]{2,1,0:T(8,128)(2,1)}, u32[]{:S(2)}) copy-start(bf16[2,128,512]{2,1,0:T(8,128)(2,1)} %param.7) | copy-start | bytes 786436
  1.9 1.1 %copy-start = (bf16[24,96,128]{2,1,0:T(8,128)(2,1)S(1)}, bf16[24,96,128]{2,1,0:T(8,128)(2,1)}, u32[]{:S(2)}) copy-start(bf16[24,96,128]{2,1,0:T(8,128)(2,1)} %param.5) | copy-start | bytes 1769476

commit v2 on v0

--- a/solution.py
+++ b/solution.py
@@ -1,7 +1,13 @@
+import functools
+
 import jax
 import jax.numpy as jnp
 from jax import lax
+from jax.experimental import pallas as pl
+from jax.experimental.pallas import tpu as pltpu
 from jax.sharding import PartitionSpec as P
+
+LANES = 128
 
 
 def layer_norm(values, dimension):
@@ -52,8 +58,434 @@
     return output.reshape(tile_rows, tile_cols, channels)
 
 
+def flip(index, step, count):
+    total, bit = 0, 1
+    while bit < count:
+        total = total + ((index // bit + step // bit) % 2) * bit
+        bit *= 2
+    return total
+
+
+def step_order(count):
+    half = count // 2
+    return [half + k // 2 if k % 2 == 0 else (k // 2 + 1) % half for k in range(count)]
+
+
+def fused_kernel(
+    rows, cols, T, W,
+    z_ref, mask_ref, win_ref, wgate_ref, wout_ref, out_ref,
+    mask_rows, mask_flat, weights0, weights1, between, normed_t, gate, mixed_t, pairs,
+    send0, near0, far0, mix0, send0m, recv0m,
+    send1, recv1, mix1, send1m, recv1m,
+    near_send, near_recv, far_send, far_recv, back0_send, back0_recv,
+    out1_send, out1_recv, back1_send, back1_recv,
+):
+    D = rows * cols
+    local = D // 2
+    count = T * W
+    part = count // 2
+    owned = recv1.shape[2] // 2
+    N = rows * T
+    per_col = N // cols
+    fours = T // 4
+    me = lax.axis_index("row") * cols + lax.axis_index("col")
+    order = step_order(D)
+    lane = lax.broadcasted_iota(jnp.int32, (1, LANES), 1)
+    chunk = 384
+
+    def device(step):
+        other = flip(me, step, D)
+        return {"row": other // cols, "col": other % cols}
+
+    def remote(source, target, sent, received, step):
+        return pltpu.make_async_remote_copy(
+            src_ref=source, dst_ref=target, send_sem=sent, recv_sem=received,
+            device_id=device(step), device_id_type=pl.DeviceIdType.MESH,
+        )
+
+    def near(t):
+        return remote(send0.at[t], near0.at[t], near_send.at[t], near_recv.at[t], t)
+
+    def far(t):
+        return remote(
+            send0.at[t, pl.ds(0, 2 * owned)], far0.at[t], far_send.at[t], far_recv.at[t], local + t
+        )
+
+    def back0(ph, t):
+        return remote(
+            send0m.at[ph, t], recv0m.at[ph, t], back0_send.at[ph, t], back0_recv.at[ph, t], t
+        )
+
+    def out1(ph, step):
+        return remote(
+            send1.at[ph, step], recv1.at[ph, step], out1_send.at[ph, step], out1_recv.at[ph, step], step
+        )
+
+    def back1(step):
+        return remote(send1m.at[step], recv1m.at[step], back1_send.at[step], back1_recv.at[step], step)
+
+    barrier = pltpu.get_barrier_semaphore()
+    for step in range(1, D):
+        pl.semaphore_signal(
+            barrier, inc=1, device_id=device(step), device_id_type=pl.DeviceIdType.MESH
+        )
+
+    def split_rows(v):
+        one = jnp.where(lane < 32, pltpu.roll(v[0], 32, 1), pltpu.roll(v[1], 32, 1))
+        two = jnp.where(lane < 64, pltpu.roll(v[1], 64, 1), pltpu.roll(v[2], 64, 1))
+        return [jnp.where(lane < W, x, 0.0) for x in (v[0], one, two, pltpu.roll(v[2], 96, 1))]
+
+    def join_rows(p):
+        one, two, three = pltpu.roll(p[1], 96, 1), pltpu.roll(p[2], 64, 1), pltpu.roll(p[3], 32, 1)
+        return [
+            jnp.where(lane < 96, p[0], one),
+            jnp.where(lane < 64, one, two),
+            jnp.where(lane < 32, two, three),
+        ]
+
+    def spread(load, half, block, begin, end):
+        for four in range(begin, end):
+            v = [load((3 * (four - begin) + i) * LANES).astype(jnp.float32) for i in range(3)]
+            for i, piece in enumerate(split_rows(v)):
+                pairs[half, block, pl.ds(4 * four + i, 2 * owned, stride=T), :] = piece
+
+    def opened(logits):
+        return 0.5 + 0.5 * jnp.tanh(0.5 * logits)
+
+    def arrange(update, target, size):
+        turned = win_ref[update].astype(jnp.float32).T
+        H = turned.shape[0] // 4
+        for owner in range(H // size):
+            target[owner] = jnp.concatenate(
+                [turned[q * H + owner * size : q * H + (owner + 1) * size] for q in range(4)], axis=0
+            ).astype(jnp.bfloat16)
+
+    def normalize(update, at, values):
+        centered = values - jnp.mean(values, axis=1, keepdims=True)
+        variance = jnp.mean(centered * centered, axis=1, keepdims=True)
+        result = centered * lax.rsqrt(variance + 1e-05)
+        normed_t[:, at] = result.T.astype(jnp.bfloat16)
+        gate[at, :] = opened(
+            jnp.dot(result.astype(jnp.bfloat16), wgate_ref[update], preferred_element_type=jnp.float32)
+        )
+
+    def normalize_input(index, carry):
+        at = pl.ds(pl.multiple_of(index * chunk, chunk), chunk)
+        normalize(0, at, z_ref[at, :].astype(jnp.float32))
+        return carry
+
+    arrange(0, weights0, 2 * owned)
+    mask_rows[...] = jnp.zeros_like(mask_rows)
+    mask_rows[:, :W] = mask_ref[...].astype(jnp.float32)
+    for four in range(fours):
+        p = [mask_rows[pl.ds(4 * four + i, 1), :] for i in range(4)]
+        for i, piece in enumerate(join_rows(p)):
+            mask_flat[:, pl.ds((3 * four + i) * LANES, LANES)] = piece
+    lax.fori_loop(0, count // chunk, normalize_input, 0)
+    pl.semaphore_wait(barrier, D - 1)
+
+    wide = 768
+    for first in range(0, local, 2):
+        steps = (first, first + 1)
+        weights = jnp.concatenate([weights0[flip(me, t, D) % local] for t in steps], axis=0)
+        for start in range(0, count, wide):
+            here = pl.ds(start, wide)
+            projected = jnp.dot(weights, normed_t[:, here], preferred_element_type=jnp.float32)
+            for place, t in enumerate(steps):
+                base = place * 8 * owned
+                gates = projected[base : base + 4 * owned]
+                values = projected[base + 4 * owned : base + 8 * owned]
+                both = (mask_flat[:, here] * opened(gates) * values).astype(jnp.bfloat16)
+                send0[t, : 2 * owned, here] = both[2 * owned :]
+                send0[t, 2 * owned :, here] = both[: 2 * owned]
+        for t in steps:
+            far(t).start()
+        for t in steps:
+            if t:
+                near(t).start()
+
+    def spread_near(ref, t):
+        source = flip(me, t, D)
+        block, half = source // cols, source % cols
+        spread(lambda at: ref[t, : 2 * owned, pl.ds(at, LANES)], half, block, 0, fours)
+        spread(
+            lambda at: ref[t, 2 * owned :, pl.ds(at, LANES)],
+            half, rows + block % (rows // 2), 0, fours,
+        )
+
+    def spread_far(t):
+        far(t).wait_recv()
+        source = flip(me, local + t, D)
+        spread(
+            lambda at: far0[t, :, pl.ds(at, LANES)], source % cols, source // cols, 0, fours
+        )
+
+    spread_near(send0, 0)
+    arrange(1, weights1, owned)
+    spread_far(0)
+
+    def receive0(t, carry):
+        near(t).wait_recv()
+        spread_near(near0, t)
+        spread_far(t)
+        return carry
+
+    lax.fori_loop(1, local, receive0, 0)
+
+    def channel(which, half, begin, blocks):
+        block = pairs[half, pl.ds(begin, blocks), pl.ds(which * T, T), :]
+        return block.reshape(blocks * T, LANES).astype(jnp.bfloat16)
+
+    for h in range(2 * owned):
+        left = jnp.concatenate(
+            [channel(h, half, rows, rows // 2) for half in range(cols)], axis=1
+        )
+        right = jnp.concatenate([channel(h, half, 0, rows) for half in range(cols)], axis=1)
+        blank = jnp.zeros((LANES - per_col, cols * LANES), jnp.bfloat16)
+        padded = []
+        for half in range(cols):
+            padded += [right[half * per_col : (half + 1) * per_col], blank]
+        product = lax.dot_general(
+            left, jnp.concatenate(padded, axis=0), (((1,), (1,)), ((), ())),
+            preferred_element_type=jnp.float32,
+        )
+        for block in range(rows // 2):
+            for half in range(cols):
+                mix0[block, half, pl.ds(h * T, T), :] = product[
+                    block * T : (block + 1) * T, half * LANES : (half + 1) * LANES
+                ]
+
+    def pack0(ph, t, target):
+        other = flip(me, t, D)
+        block, half = other // cols % (rows // 2), other % cols
+        for four in range(fours // 2):
+            row = ph * (T // 2) + 4 * four
+            p = [mix0[block, half, pl.ds(row + i, 2 * owned, stride=T), :] for i in range(4)]
+            for i, piece in enumerate(join_rows(p)):
+                target[ph, t, :, pl.ds((3 * four + i) * LANES, LANES)] = piece.astype(jnp.bfloat16)
+
+    for ph in range(2):
+        def give0(t, carry):
+            pack0(ph, t, send0m)
+            back0(ph, t).start()
+            return carry
+
+        lax.fori_loop(1, local, give0, 0)
+        pack0(ph, 0, recv0m)
+
+    def mixed_update(update, at):
+        values = mixed_t[:, at]
+        centered = values - jnp.mean(values, axis=0, keepdims=True)
+        variance = jnp.mean(centered * centered, axis=0, keepdims=True)
+        mixed_norm = (centered * lax.rsqrt(variance + 1e-05)).T.astype(jnp.bfloat16)
+        return gate[at, :] * jnp.dot(
+            mixed_norm, wout_ref[update], preferred_element_type=jnp.float32
+        )
+
+    bundle = 4
+    for ph in range(2):
+        span = pl.ds(ph * part, part)
+
+        def collect0(t):
+            owner = flip(me, t, D) % local
+            at = pl.ds(pl.multiple_of(owner * 2 * owned, 2 * owned), 2 * owned)
+            mixed_t[at, span] = recv0m[ph, t].astype(jnp.float32)
+
+        def take0(t, carry):
+            back0(ph, t).wait_recv()
+            collect0(t)
+            return carry
+
+        collect0(0)
+        lax.fori_loop(1, local, take0, 0)
+
+        def finish0(index, carry):
+            at = pl.ds(pl.multiple_of(ph * part + index * chunk, chunk), chunk)
+            result = (z_ref[at, :].astype(jnp.float32) + mixed_update(0, at)).astype(jnp.bfloat16)
+            between[at, :] = result
+            normalize(1, at, result.astype(jnp.float32))
+            return carry
+
+        lax.fori_loop(0, part // chunk, finish0, 0)
+        for first in range(0, D, bundle):
+            steps = order[first : first + bundle]
+            weights = jnp.concatenate([weights1[flip(me, step, D)] for step in steps], axis=0)
+            for start in range(0, part, chunk):
+                here = pl.ds(ph * part + start, chunk)
+                projected = jnp.dot(weights, normed_t[:, here], preferred_element_type=jnp.float32)
+                for place, step in enumerate(steps):
+                    base = place * 4 * owned
+                    gates = projected[base : base + 2 * owned]
+                    values = projected[base + 2 * owned : base + 4 * owned]
+                    target = recv1 if step == 0 else send1
+                    target[ph, step, :, pl.ds(start, chunk)] = (
+                        mask_flat[:, here] * opened(gates) * values
+                    ).astype(jnp.bfloat16)
+            for step in steps:
+                if step:
+                    out1(ph, step).start()
+
+    def at_order(k):
+        return jnp.where(k % 2 == 0, local + k // 2, (k // 2 + 1) % local)
+
+    for ph in range(2):
+        def spread1(step):
+            source = flip(me, step, D)
+            spread(
+                lambda at: recv1[ph, step, :, pl.ds(at, LANES)],
+                source % cols, source // cols, ph * (fours // 2), (ph + 1) * (fours // 2),
+            )
+
+        def receive1(k, carry):
+            step = at_order(k)
+            out1(ph, step).wait_recv()
+            spread1(step)
+            return carry
+
+        spread1(0)
+        lax.fori_loop(0, D - 1, receive1, 0)
+
+    for h in range(owned):
+        left = jnp.concatenate([channel(h, half, 0, rows) for half in range(cols)], axis=1)
+        right = jnp.concatenate([channel(owned + h, half, 0, rows) for half in range(cols)], axis=1)
+        product = lax.dot_general(
+            left, right, (((0,), (0,)), ((), ())), preferred_element_type=jnp.float32
+        )
+        for block in range(rows):
+            at = block * T // per_col * LANES + block * T % per_col
+            for half in range(cols):
+                mix1[block, half, pl.ds(h * T, T), :] = product[
+                    at : at + T, half * LANES : (half + 1) * LANES
+                ]
+
+    def pack1(step, target):
+        other = flip(me, step, D)
+        block, half = other // cols, other % cols
+        for four in range(fours // 2):
+            both = [
+                join_rows([
+                    mix1[block, half, pl.ds(ph * (T // 2) + 4 * four + i, owned, stride=T), :]
+                    for i in range(4)
+                ])
+                for ph in range(2)
+            ]
+            for i in range(3):
+                target[step, :, pl.ds((3 * four + i) * LANES, LANES)] = jnp.concatenate(
+                    [both[0][i], both[1][i]], axis=0
+                ).astype(jnp.bfloat16)
+
+    def give1(k, carry):
+        step = at_order(k)
+        pack1(step, send1m)
+        back1(step).start()
+        return carry
+
+    lax.fori_loop(0, D - 1, give1, 0)
+    pack1(0, recv1m)
+
+    def collect1(step):
+        owner = flip(me, step, D)
+        at = pl.ds(pl.multiple_of(owner * owned, owned), owned)
+        values = recv1m[step].astype(jnp.float32)
+        mixed_t[at, :part] = values[:owned]
+        mixed_t[at, part:] = values[owned:]
+
+    def take1(k, carry):
+        step = at_order(k)
+        back1(step).wait_recv()
+        collect1(step)
+        return carry
+
+    collect1(0)
+    lax.fori_loop(0, D - 1, take1, 0)
+
+    def finish1(index, carry):
+        at = pl.ds(pl.multiple_of(index * chunk, chunk), chunk)
+        out_ref[at, :] = (between[at, :].astype(jnp.float32) + mixed_update(1, at)).astype(jnp.bfloat16)
+        return carry
+
+    lax.fori_loop(0, count // chunk, finish1, 0)
+
+    far(0).wait_send()
+
+    def settle0(t, carry):
+        far(t).wait_send()
+        near(t).wait_send()
+        back0(0, t).wait_send()
+        back0(1, t).wait_send()
+        return carry
+
+    def settle1(step, carry):
+        out1(0, step).wait_send()
+        out1(1, step).wait_send()
+        back1(step).wait_send()
+        return carry
+
+    lax.fori_loop(1, local, settle0, 0)
+    lax.fori_loop(1, D, settle1, 0)
+
+
+def fused_updates(flat, mask, w_in, w_gate, w_out):
+    rows, cols = lax.axis_size("row"), lax.axis_size("col")
+    D = rows * cols
+    local = D // 2
+    T, W = mask.shape
+    count, C = flat.shape
+    owned = w_in.shape[2] // 4 // D
+    vmem, half, full = pltpu.VMEM, jnp.bfloat16, jnp.float32
+    dma = pltpu.SemaphoreType.DMA
+    return pl.pallas_call(
+        functools.partial(fused_kernel, rows, cols, T, W),
+        out_shape=jax.ShapeDtypeStruct((count, C), half),
+        in_specs=[pl.BlockSpec(memory_space=vmem)] * 5,
+        out_specs=pl.BlockSpec(memory_space=vmem),
+        scratch_shapes=[
+            vmem((T, LANES), full),
+            vmem((1, count), full),
+            vmem((local, 8 * owned, C), half),
+            vmem((D, 4 * owned, C), half),
+            vmem((count, C), half),
+            vmem((C, count), half),
+            vmem((count, C), full),
+            vmem((D * owned, count), full),
+            vmem((cols, rows + rows // 2, 2 * owned * T, LANES), full),
+            vmem((local, 4 * owned, count), half),
+            vmem((local, 4 * owned, count), half),
+            vmem((local, 2 * owned, count), half),
+            vmem((rows // 2, cols, 2 * owned * T, LANES), full),
+            vmem((2, local, 2 * owned, count // 2), half),
+            vmem((2, local, 2 * owned, count // 2), half),
+            vmem((2, D, 2 * owned, count // 2), half),
+            vmem((2, D, 2 * owned, count // 2), half),
+            vmem((rows, cols, owned * T, LANES), full),
+            vmem((D, 2 * owned, count // 2), half),
+            vmem((D, 2 * owned, count // 2), half),
+            dma((local,)), dma((local,)), dma((local,)), dma((local,)),
+            dma((2, local)), dma((2, local)),
+            dma((2, D)), dma((2, D)), dma((D,)), dma((D,)),
+        ],
+        compiler_params=pltpu.CompilerParams(
+            collective_id=0, has_side_effects=True, vmem_limit_bytes=48 * 1024 * 1024
+        ),
+    )(flat, mask, w_in, w_gate, w_out)
+
+
+def fits_fused(pair, w_in):
+    rows, cols = lax.axis_size("row"), lax.axis_size("col")
+    D = rows * cols
+    T, W, C = pair.shape
+    H = w_in.shape[2] // 4
+    return (
+        W == 96 and T % 8 == 0 and cols == 2 and D & (D - 1) == 0
+        and C == LANES and H == LANES and H == 8 * D and rows * T == cols * W
+    )
+
+
 def per_device(pair, mask, w_in, w_gate, w_out):
     mask_flat = mask.reshape(-1).astype(jnp.float32)
+    if fits_fused(pair, w_in):
+        T, W, C = pair.shape
+        return fused_updates(pair.reshape(T * W, C), mask, w_in, w_gate, w_out).reshape(T, W, C)
     first = triangle(pair, mask_flat, w_in[0], w_gate[0], w_out[0], True)
     return triangle(first, mask_flat, w_in[1], w_gate[1], w_out[1], False)
 

time: 147 us -> 94.5 us (0.64)
  Pallas kernels: 0 us -> 88.9 us
  blocking collectives: 70.3 us -> 0 us
  waiting for transfers between devices: 29.5 us -> 0 us
  local copies, waits for them, and re-layouts: 24.1 us -> 5.21 us
  matrix products: 7.81 us -> 0 us
  starting transfers between devices: 7.35 us -> 0 us
  other arithmetic: 6.64 us -> 0 us
    pallas_call x0 -> x1, Pallas kernels: none -> 88.9 us  [fused_updates(): pl.pallas_call(functools.partial(fused_kernel, rows, cols, T, W), out_sha...]
    all_to_all x2 -> x0, blocking collectives: 70.3 us -> none  [triangle(): lax.all_to_all(stacked, ('row', 'col'), split_axis=1, concat_axis=1, tile...]
    all_to_all x2 -> x0, waiting for transfers between devices: 29.5 us -> none  [triangle(): lax.all_to_all(product.reshape(groups, item_count, pair_count), ('row', '...]
    reshape x11 -> x0, local copies, waits for them, and re-layouts: 14.5 us -> none  [the longest x3 8.4 us: triangle(): pieces.reshape(2, row_count, col_count, item_count, tile_rows, tile_cols)]
    dot_general x8 -> x0, matrix products: 7.81 us -> none  [the longest x2 2.88 us: triangle(): jnp.einsum(equation, gathered[0], gathered[1], preferred_element_type=jnp...]
    all_to_all x2 -> x0, starting transfers between devices: 7.35 us -> none  [triangle(): lax.all_to_all(product.reshape(groups, item_count, pair_count), ('row', '...]
    reduce_sum x7 -> x0, other arithmetic: 4.52 us -> none  [the longest x4 2.91 us: layer_norm(): variance = jnp.mean(centered * centered, axis=dimension, keepdims=True)]
    unnamed x24 -> x11, local copies, waits for them, and re-layouts: 0.81 us -> 5.21 us
  transfers between devices with their start and end apart: 2 -> 0, of which waited for: 2 -> 0; matrix products, arithmetic and copies ran while one was open for 1% -> 0% of each run, Pallas kernels for 0% -> 0%
where the time goes in v2:
time: 94.5 us; the launch traced here: 94.2 us
  Pallas kernels  88.9 us (94%)
  local copies, waits for them, and re-layouts  5.21 us (6%)
    pallas_call x1, Pallas kernels, fused_updates(): pl.pallas_call(functools.partial(fused_kernel, rows, cols, T, W), out_sha...  88.9 us
    unnamed x11, local copies, waits for them, and re-layouts  5.21 us

profile of v2, /device:TPU:0, one launch (start us, length us, event | category | flops | bytes accessed | tf_op | source)
XLA Modules:
  0.0 94.2 jit_solution(5525746902911694688)
XLA Ops:
  0.0 0.0 copy-start
  0.0 1.1 %copy-done = bf16[24,96,128]{2,1,0:T(8,128)(2,1)S(1)} copy-done((bf16[24,96,128]{2,1,0:T(8,128)(2,1)S(1)}, bf16[24,96,128]{2,1,0:T(8,128)(2,1)}, u32[]{:S(2)}) %copy-start) | copy-done | bytes 589848
  1.1 0.0 copy-start.1
  1.1 0.9 %copy-done.1 = bf16[2,128,512]{2,1,0:T(8,128)(2,1)S(1)} copy-done((bf16[2,128,512]{2,1,0:T(8,128)(2,1)S(1)}, bf16[2,128,512]{2,1,0:T(8,128)(2,1)}, u32[]{:S(2)}) %copy-start.1) | copy-done | bytes 262168
  2.0 0.0 copy-start.2
  2.0 0.8 copy-done.2
  2.9 0.0 copy-start.3
  2.9 0.8 copy-done.3
  3.7 0.0 copy-start.4
  3.7 0.7 copy-done.4
  4.4 88.9 %shard_map.55 = bf16[2304,128]{1,0:T(8,128)(2,1)S(1)} custom-call(bf16[2304,128]{1,0:T(8,128)(2,1)S(1)} %bitcast.3, s32[24,96]{1,0:T(8,128)S(1)} %copy-done.4, bf16[2,128,512]{2,1,0:T(8,128)(2,1)S(1)} %copy-done.1, bf16[2,128,128]{2,1,0:T(8,128)(2,1)S(1)} %copy-done.2, bf16[2,128,128]{2,1,0:T(8,128)(2,1)S(1)} %copy-done.3), custom_call_target="tpu_custom_call" | custom-call | tf_op jit(solution)/shard_map/pallas_call | solution.py:437
  93.4 0.8 copy.7
Async XLA Ops:
  0.0 1.1 %copy-start = (bf16[24,96,128]{2,1,0:T(8,128)(2,1)S(1)}, bf16[24,96,128]{2,1,0:T(8,128)(2,1)}, u32[]{:S(2)}) copy-start(bf16[24,96,128]{2,1,0:T(8,128)(2,1)} %param.5) | copy-start | bytes 1769476
  1.1 0.9 %copy-start.1 = (bf16[2,128,512]{2,1,0:T(8,128)(2,1)S(1)}, bf16[2,128,512]{2,1,0:T(8,128)(2,1)}, u32[]{:S(2)}) copy-start(bf16[2,128,512]{2,1,0:T(8,128)(2,1)} %win_ref.1) | copy-start | bytes 786436
  2.0 0.8 copy-start.2
  2.9 0.8 copy-start.3
  3.7 0.7 copy-start.4

commit v3 on v2

--- a/solution.py
+++ b/solution.py
@@ -73,8 +73,8 @@
 
 def fused_kernel(
     rows, cols, T, W,
-    z_ref, mask_ref, win_ref, wgate_ref, wout_ref, out_ref,
-    mask_rows, mask_flat, weights0, weights1, between, normed_t, gate, mixed_t, pairs,
+    z_hbm, mask_hbm, win_hbm, wgate_hbm, wout_hbm, out_ref,
+    z_ref, mask_ref, win_ref, wgate_ref, wout_ref, load_sem, normed, mask_rows, mask_flat, weights0, weights1, between, normed_t, gate, mixed_t, pairs,
     send0, near0, far0, mix0, send0m, recv0m,
     send1, recv1, mix1, send1m, recv1m,
     near_send, near_recv, far_send, far_recv, back0_send, back0_recv,
@@ -124,6 +124,15 @@
     def back1(step):
         return remote(send1m.at[step], recv1m.at[step], back1_send.at[step], back1_recv.at[step], step)
 
+    loads = [
+        pltpu.make_async_copy(source, target, load_sem.at[i])
+        for i, (source, target) in enumerate([
+            (win_hbm, win_ref), (z_hbm, z_ref), (mask_hbm, mask_ref),
+            (wgate_hbm, wgate_ref), (wout_hbm, wout_ref),
+        ])
+    ]
+    for load in loads:
+        load.start()
     barrier = pltpu.get_barrier_semaphore()
     for step in range(1, D):
         pl.semaphore_signal(
@@ -165,8 +174,12 @@
         variance = jnp.mean(centered * centered, axis=1, keepdims=True)
         result = centered * lax.rsqrt(variance + 1e-05)
         normed_t[:, at] = result.T.astype(jnp.bfloat16)
+        normed[at, :] = result.astype(jnp.bfloat16)
+
+    def open_gate(update, index):
+        at = pl.ds(pl.multiple_of(index * chunk, chunk), chunk)
         gate[at, :] = opened(
-            jnp.dot(result.astype(jnp.bfloat16), wgate_ref[update], preferred_element_type=jnp.float32)
+            jnp.dot(normed[at, :], wgate_ref[update], preferred_element_type=jnp.float32)
         )
 
     def normalize_input(index, carry):
@@ -174,19 +187,29 @@
         normalize(0, at, z_ref[at, :].astype(jnp.float32))
         return carry
 
+    def open_gates(update):
+        def one(index, carry):
+            open_gate(update, index)
+            return carry
+
+        lax.fori_loop(0, count // chunk, one, 0)
+
+    loads[0].wait()
     arrange(0, weights0, 2 * owned)
+    loads[1].wait()
+    lax.fori_loop(0, count // chunk, normalize_input, 0)
+    loads[2].wait()
     mask_rows[...] = jnp.zeros_like(mask_rows)
     mask_rows[:, :W] = mask_ref[...].astype(jnp.float32)
     for four in range(fours):
         p = [mask_rows[pl.ds(4 * four + i, 1), :] for i in range(4)]
         for i, piece in enumerate(join_rows(p)):
             mask_flat[:, pl.ds((3 * four + i) * LANES, LANES)] = piece
-    lax.fori_loop(0, count // chunk, normalize_input, 0)
     pl.semaphore_wait(barrier, D - 1)
 
     wide = 768
-    for first in range(0, local, 2):
-        steps = (first, first + 1)
+    for first in range(local // 2):
+        steps = (first, local // 2 + first)
         weights = jnp.concatenate([weights0[flip(me, t, D) % local] for t in steps], axis=0)
         for start in range(0, count, wide):
             here = pl.ds(start, wide)
@@ -220,11 +243,15 @@
             lambda at: far0[t, :, pl.ds(at, LANES)], source % cols, source // cols, 0, fours
         )
 
+    loads[3].wait()
+    loads[4].wait()
+    open_gates(0)
     spread_near(send0, 0)
     arrange(1, weights1, owned)
     spread_far(0)
 
-    def receive0(t, carry):
+    def receive0(k, carry):
+        t = k // 2 + k % 2 * (local // 2)
         near(t).wait_recv()
         spread_near(near0, t)
         spread_far(t)
@@ -265,7 +292,8 @@
                 target[ph, t, :, pl.ds((3 * four + i) * LANES, LANES)] = piece.astype(jnp.bfloat16)
 
     for ph in range(2):
-        def give0(t, carry):
+        def give0(k, carry):
+            t = k // 2 + k % 2 * (local // 2)
             pack0(ph, t, send0m)
             back0(ph, t).start()
             return carry
@@ -291,7 +319,8 @@
             at = pl.ds(pl.multiple_of(owner * 2 * owned, 2 * owned), 2 * owned)
             mixed_t[at, span] = recv0m[ph, t].astype(jnp.float32)
 
-        def take0(t, carry):
+        def take0(k, carry):
+            t = k // 2 + k % 2 * (local // 2)
             back0(ph, t).wait_recv()
             collect0(t)
             return carry
@@ -325,6 +354,8 @@
                 if step:
                     out1(ph, step).start()
 
+    open_gates(1)
+
     def at_order(k):
         return jnp.where(k % 2 == 0, local + k // 2, (k // 2 + 1) % local)
 
@@ -437,9 +468,16 @@
     return pl.pallas_call(
         functools.partial(fused_kernel, rows, cols, T, W),
         out_shape=jax.ShapeDtypeStruct((count, C), half),
-        in_specs=[pl.BlockSpec(memory_space=vmem)] * 5,
+        in_specs=[pl.BlockSpec(memory_space=pltpu.HBM)] * 5,
         out_specs=pl.BlockSpec(memory_space=vmem),
         scratch_shapes=[
+            vmem(flat.shape, half),
+            vmem(mask.shape, jnp.int32),
+            vmem(w_in.shape, half),
+            vmem(w_gate.shape, half),
+            vmem(w_out.shape, half),
+            dma((5,)),
+            vmem((count, C), half),
             vmem((T, LANES), full),
             vmem((1, count), full),
             vmem((local, 8 * owned, C), half),
@@ -465,7 +503,7 @@
             dma((2, D)), dma((2, D)), dma((D,)), dma((D,)),
         ],
         compiler_params=pltpu.CompilerParams(
-            collective_id=0, has_side_effects=True, vmem_limit_bytes=48 * 1024 * 1024
+            collective_id=0, has_side_effects=True, vmem_limit_bytes=64 * 1024 * 1024
         ),
     )(flat, mask, w_in, w_gate, w_out)
 

time: 94.5 us -> 91.4 us (0.967); the launches traced: 94.2 us -> 90.1 us
  local copies, waits for them, and re-layouts: 5.21 us -> 1.92 us
    unnamed x11 -> x1, local copies, waits for them, and re-layouts: 5.21 us -> 1.92 us
where the time goes in v3:
time: 91.4 us; the launch traced here: 90.1 us
  Pallas kernels  88.2 us (96%)
  local copies, waits for them, and re-layouts  1.92 us (2%)
    pallas_call x1, Pallas kernels, fused_updates(): pl.pallas_call(functools.partial(fused_kernel, rows, cols, T, W), out_sha...  88.2 us
    unnamed x1, local copies, waits for them, and re-layouts  1.92 us

profile of v3, /device:TPU:0, one launch (start us, length us, event | category | flops | bytes accessed | tf_op | source)
XLA Modules:
  0.0 90.1 jit_solution(6737825452566859824)
XLA Ops:
  0.0 88.2 %shard_map.55 = bf16[2304,128]{1,0:T(8,128)(2,1)} custom-call(bf16[2304,128]{1,0:T(8,128)(2,1)} %bitcast.3, s32[24,96]{1,0:T(8,128)} %mask_hbm.1, bf16[2,128,512]{2,1,0:T(8,128)(2,1)} %win_hbm.1, bf16[2,128,128]{2,1,0:T(8,128)(2,1)} %wgate_hbm.1, bf16[2,128,128]{2,1,0:T(8,128)(2,1)} %wout_hbm.1), custom_call_target="tpu_custom_call" | custom-call | tf_op jit(solution)/shard_map/pallas_call | solution.py:468
  88.2 1.9 %copy.7 = bf16[24,96,128]{2,1,0:T(8,128)(2,1)} copy(bf16[24,96,128]{2,1,0:T(8,128)(2,1)} %bitcast.2) | data formatting | bytes 1179648

commit v4 on v3

--- a/solution.py
+++ b/solution.py
@@ -121,8 +121,11 @@
             send1.at[ph, step], recv1.at[ph, step], out1_send.at[ph, step], out1_recv.at[ph, step], step
         )
 
-    def back1(step):
-        return remote(send1m.at[step], recv1m.at[step], back1_send.at[step], back1_recv.at[step], step)
+    def back1(four, step):
+        return remote(
+            send1m.at[four, step], recv1m.at[four, step],
+            back1_send.at[four, step], back1_recv.at[four, step], step,
+        )
 
     loads = [
         pltpu.make_async_copy(source, target, load_sem.at[i])
@@ -389,53 +392,52 @@
                     at : at + T, half * LANES : (half + 1) * LANES
                 ]
 
-    def pack1(step, target):
+    def pack1(four, step, target):
         other = flip(me, step, D)
         block, half = other // cols, other % cols
-        for four in range(fours // 2):
-            both = [
-                join_rows([
-                    mix1[block, half, pl.ds(ph * (T // 2) + 4 * four + i, owned, stride=T), :]
-                    for i in range(4)
-                ])
-                for ph in range(2)
-            ]
-            for i in range(3):
-                target[step, :, pl.ds((3 * four + i) * LANES, LANES)] = jnp.concatenate(
-                    [both[0][i], both[1][i]], axis=0
-                ).astype(jnp.bfloat16)
-
-    def give1(k, carry):
-        step = at_order(k)
-        pack1(step, send1m)
-        back1(step).start()
-        return carry
-
-    lax.fori_loop(0, D - 1, give1, 0)
-    pack1(0, recv1m)
-
-    def collect1(step):
-        owner = flip(me, step, D)
-        at = pl.ds(pl.multiple_of(owner * owned, owned), owned)
-        values = recv1m[step].astype(jnp.float32)
-        mixed_t[at, :part] = values[:owned]
-        mixed_t[at, part:] = values[owned:]
-
-    def take1(k, carry):
-        step = at_order(k)
-        back1(step).wait_recv()
-        collect1(step)
-        return carry
-
-    collect1(0)
-    lax.fori_loop(0, D - 1, take1, 0)
-
-    def finish1(index, carry):
-        at = pl.ds(pl.multiple_of(index * chunk, chunk), chunk)
-        out_ref[at, :] = (between[at, :].astype(jnp.float32) + mixed_update(1, at)).astype(jnp.bfloat16)
-        return carry
-
-    lax.fori_loop(0, count // chunk, finish1, 0)
+        both = [
+            join_rows([
+                mix1[block, half, pl.ds(ph * (T // 2) + 4 * four + i, owned, stride=T), :]
+                for i in range(4)
+            ])
+            for ph in range(2)
+        ]
+        for i in range(3):
+            target[four, step, :, pl.ds(i * LANES, LANES)] = jnp.concatenate(
+                [both[0][i], both[1][i]], axis=0
+            ).astype(jnp.bfloat16)
+
+    for four in range(fours // 2):
+        def give1(k, carry):
+            step = at_order(k)
+            pack1(four, step, send1m)
+            back1(four, step).start()
+            return carry
+
+        lax.fori_loop(0, D - 1, give1, 0)
+        pack1(four, 0, recv1m)
+
+    for four in range(fours // 2):
+        def collect1(step):
+            owner = flip(me, step, D)
+            at = pl.ds(pl.multiple_of(owner * owned, owned), owned)
+            values = recv1m[four, step].astype(jnp.float32)
+            mixed_t[at, pl.ds(four * chunk, chunk)] = values[:owned]
+            mixed_t[at, pl.ds(part + four * chunk, chunk)] = values[owned:]
+
+        def take1(k, carry):
+            step = at_order(k)
+            back1(four, step).wait_recv()
+            collect1(step)
+            return carry
+
+        collect1(0)
+        lax.fori_loop(0, D - 1, take1, 0)
+        for ph in range(2):
+            at = pl.ds(ph * part + four * chunk, chunk)
+            out_ref[at, :] = (
+                between[at, :].astype(jnp.float32) + mixed_update(1, at)
+            ).astype(jnp.bfloat16)
 
     far(0).wait_send()
 
@@ -449,7 +451,8 @@
     def settle1(step, carry):
         out1(0, step).wait_send()
         out1(1, step).wait_send()
-        back1(step).wait_send()
+        for four in range(fours // 2):
+            back1(four, step).wait_send()
         return carry
 
     lax.fori_loop(1, local, settle0, 0)
@@ -496,11 +499,11 @@
             vmem((2, D, 2 * owned, count // 2), half),
             vmem((2, D, 2 * owned, count // 2), half),
             vmem((rows, cols, owned * T, LANES), full),
-            vmem((D, 2 * owned, count // 2), half),
-            vmem((D, 2 * owned, count // 2), half),
+            vmem((T // 8, D, 2 * owned, 4 * W), half),
+            vmem((T // 8, D, 2 * owned, 4 * W), half),
             dma((local,)), dma((local,)), dma((local,)), dma((local,)),
             dma((2, local)), dma((2, local)),
-            dma((2, D)), dma((2, D)), dma((D,)), dma((D,)),
+            dma((2, D)), dma((2, D)), dma((T // 8, D)), dma((T // 8, D)),
         ],
         compiler_params=pltpu.CompilerParams(
             collective_id=0, has_side_effects=True, vmem_limit_bytes=64 * 1024 * 1024
@@ -514,7 +517,7 @@
     T, W, C = pair.shape
     H = w_in.shape[2] // 4
     return (
-        W == 96 and T % 8 == 0 and cols == 2 and D & (D - 1) == 0
+        W == 96 and T == 24 and cols == 2 and D & (D - 1) == 0
         and C == LANES and H == LANES and H == 8 * D and rows * T == cols * W
     )
 

time: 91.4 us -> 92.2 us (level); the launches traced: 90.1 us -> 92 us
  Pallas kernels: 88.2 us -> 90.1 us
    pallas_call x1, Pallas kernels: 88.2 us -> 90.1 us  [fused_updates(): pl.pallas_call(functools.partial(fused_kernel, rows, cols, T, W), out_sha...]
where the time goes in v4:
time: 92.2 us; the launch traced here: 92 us
  Pallas kernels  90.1 us (98%)
  local copies, waits for them, and re-layouts  1.92 us (2%)
    pallas_call x1, Pallas kernels, fused_updates(): pl.pallas_call(functools.partial(fused_kernel, rows, cols, T, W), out_sha...  90.1 us
    unnamed x1, local copies, waits for them, and re-layouts  1.92 us

profile of v4, /device:TPU:0, one launch (start us, length us, event | category | flops | bytes accessed | tf_op | source)
XLA Modules:
  0.0 92.0 jit_solution(5762375117877382165)
XLA Ops:
  0.0 90.1 %shard_map.55 = bf16[2304,128]{1,0:T(8,128)(2,1)} custom-call(bf16[2304,128]{1,0:T(8,128)(2,1)} %bitcast.3, s32[24,96]{1,0:T(8,128)} %mask_hbm.1, bf16[2,128,512]{2,1,0:T(8,128)(2,1)} %win_hbm.1, bf16[2,128,128]{2,1,0:T(8,128)(2,1)} %wgate_hbm.1, bf16[2,128,128]{2,1,0:T(8,128)(2,1)} %wout_hbm.1), custom_call_target="tpu_custom_call" | custom-call | tf_op jit(solution)/shard_map/pallas_call | solution.py:471
  90.1 1.9 %copy.7 = bf16[24,96,128]{2,1,0:T(8,128)(2,1)} copy(bf16[24,96,128]{2,1,0:T(8,128)(2,1)} %bitcast.2) | data formatting | bytes 1179648
